TPU v7x, 32 devices: a whole 2x2x4 slice. The times are simulated.
32 devices in a mesh: asc: 8 (over y, x, core), desc: 4 (over z).
Axes of the slice: x: 2, y: 2, z: 4, core: 2. Of those that a mesh axis runs over, the one named last changes fastest.
Arguments:
- coef_asc: float32 [1024, 128], P(('asc', 'desc')), may hold values from -0.3 to 0.3
- coef_desc: float32 [1024, 128], P(('asc', 'desc')), may hold values from -0.3 to 0.3
- cross_asc: int32 [2048, 128], P(('asc', 'desc')), may hold values from 0 to 1023, as said below
- cross_desc: int32 [2048, 128], P(('asc', 'desc')), may hold values from 0 to 1023, as said below
- time_asc: float32 [2048, 128], P(('asc', 'desc')), may hold values from 0 to 1
- time_desc: float32 [2048, 128], P(('asc', 'desc')), may hold values from 0 to 1
- height: float32 [2048, 128], P(('asc', 'desc')), may hold values from -18 to 18
- block_fill: int32 [2048], P(('asc', 'desc')), may hold values from 0 to 128, as said below
Outputs:
- adjusted_asc: float32 [1024, 128], P(('asc', 'desc'))
- adjusted_desc: float32 [1024, 128], P(('asc', 'desc'))
Inputs may be any that keep to these rules, and one draw needn't show every extreme that they name: `cross_asc`: every crossover slot stored on a device of asc index p names an ascending arc a with a // 128 == p; slot s of every block names an arc a with (a // 32) % 4 == s % 4. `cross_desc`: every crossover slot stored on a device of desc index q names a descending arc d with (d // 32) % 4 == q; slot s of every block names an arc d with d // 128 == s % 8. `block_fill`: the slots in use stand first in each block; on each device the blocks with a nonzero count stand first and the first block is full; on some device all 64 blocks are in use.
All inputs are finite; a program needn't handle non-finite values.
Results may differ from a plain program's by a relative error of at most 0.0003.
Values sent between devices are 32-bit elements; how exact they have to be, the bound alone decides.
No kernel may reach another device: no remote copies, remote signals or barrier semaphores. Data moves between devices by JAX's collectives and lax.ppermute only.
A program may use at most 64 MiB of HBM per device.

v0:
```python
import functools
import math

import jax
import jax.numpy as jnp
from jax import lax
from jax.experimental import pallas as pl
from jax.experimental.pallas import tpu as pltpu
from jax.sharding import PartitionSpec as P

GN_STEPS = 2
damping = 2.0
cauchy_square = 2.25

LANES = 128
STEP_ROWS = 2
UNROLL = 3
BLOCK_ROWS = STEP_ROWS * UNROLL
STEP_LANES = STEP_ROWS * LANES
DUMMY_ROWS = 8
TURNS = (5, 2, 1)
SCALE = 1.0 / 128.0
FIELDS = 5
PIVOT_FLOOR = 1e-6
F32 = jnp.float32
BF16 = jnp.bfloat16

COS_TERMS = [(-1.0) ** i * math.pi ** (2 * i) / math.factorial(2 * i) for i in range(8)]
SIN_TERMS = [(-1.0) ** i * math.pi ** (2 * i + 1) / math.factorial(2 * i + 1) for i in range(7)]


def params(mebibytes):
    return pltpu.CompilerParams(vmem_limit_bytes=mebibytes * 1024 * 1024)


def place(x):
    return pl.BlockSpec(memory_space=pltpu.VMEM)


def split(x):
    high = x.astype(BF16)
    low = (x - high.astype(F32)).astype(BF16)
    return high, low


def flat_first(ref, field, fold, rows):
    parts = []
    for j in range(ref.shape[0] * fold):
        start = (j % fold * FIELDS + field) * rows
        parts.append(ref[j // fold, start : start + rows])
    return jnp.concatenate(parts, axis=0)


def flat_second(ref, field, rows):
    start = field * rows
    return jnp.concatenate([ref[j, start : start + rows] for j in range(ref.shape[0])], axis=0)


def flat(ref, field, chunks):
    return jnp.concatenate([ref[j, field] for j in range(chunks)], axis=0)


def local_id(ids, owned):
    if owned & (owned - 1) == 0:
        return ids & (owned - 1)
    return lax.rem(ids, owned)


def pack_kernel(
    na, nd, owned_asc, coef_in, ca_in, cd_in, ta_in, td_in, height_in, fill_in, out,
    coef, ca, cd, ta, td, height, fill, turned, sems,
):
    copies = [
        pltpu.make_async_copy(source, target, sems.at[i])
        for i, (source, target) in enumerate(
            [
                (fill_in, fill), (ca_in, ca), (ta_in, ta),
                (cd_in, cd), (td_in, td), (height_in, height), (coef_in, coef),
            ]
        )
    ]
    for copy in copies:
        copy.start()
    for copy in copies:
        copy.wait()
    owned_desc = coef.shape[0]
    blocks, width = ca.shape
    group = width // na
    rows = blocks // na
    fill_row = fill[...]
    row_id = lax.broadcasted_iota(jnp.int32, (blocks, blocks), 0)
    col_id = lax.broadcasted_iota(jnp.int32, (blocks, blocks), 1)
    fill_col = jnp.sum(
        jnp.where(row_id == col_id, fill_row, 0).astype(F32), axis=1, keepdims=True
    )
    lane = lax.broadcasted_iota(jnp.int32, (blocks, width), 1)
    live = lane.astype(F32) < fill_col
    fields = [
        lambda: jnp.where(live, local_id(ca[...], owned_asc).astype(F32), -1.0),
        lambda: ta[...],
        lambda: jnp.where(live, local_id(cd[...], owned_desc).astype(F32), -1.0),
        lambda: td[...],
        lambda: height[...],
    ]
    source = lax.broadcasted_iota(jnp.int32, (width, width), 0)
    target = lax.broadcasted_iota(jnp.int32, (width, width), 1)
    owner = target // group
    place = target - owner * group
    order = (source == place * na + owner).astype(F32).astype(BF16)
    for f, field in enumerate(fields):
        x = field()
        high = x.astype(BF16)
        rest = x - high.astype(F32)
        middle = rest.astype(BF16)
        low = (rest - middle.astype(F32)).astype(BF16)
        turned[f] = (
            jnp.dot(high, order, preferred_element_type=F32)
            + jnp.dot(middle, order, preferred_element_type=F32)
        ) + jnp.dot(low, order, preferred_element_type=F32)
    lane_group = lax.broadcasted_iota(jnp.int32, (rows, width), 1) // group
    for f in range(FIELDS):
        parts = [None] * na
        for k in range(na):
            piece = turned[f, pl.ds(k, rows, stride=na), :]
            for r in range(na):
                amount = ((k - r) * group) % width
                moved = pltpu.roll(piece, amount, 1) if amount else piece
                parts[r] = moved if k == 0 else jnp.where(lane_group == k, moved, parts[r])
        for r in range(na):
            start = (r // nd * FIELDS + f) * rows
            out[r % nd, start : start + rows] = parts[r]
    for q in range(nd):
        out[q, out.shape[1] - owned_desc :] = coef[...]


def cos_sin_pi(x):
    turns = jnp.floor(x + 0.5)
    f = x - turns
    sign = 1.0 - 2.0 * (turns - 2.0 * jnp.floor(turns * 0.5))
    u = f * f
    c = COS_TERMS[-1]
    for term in COS_TERMS[-2::-1]:
        c = c * u + term
    s = SIN_TERMS[-1]
    for term in SIN_TERMS[-2::-1]:
        s = s * u + term
    return c * sign, s * (f * sign)


def rows_pair(ref, rows):
    return jnp.concatenate([ref[pl.ds(r, 1), :] for r in rows], axis=1)


def used_rows(ids_ref, chunks, rows, table):
    count = jnp.int32(0)
    level = lax.broadcasted_iota(jnp.int32, (rows, LANES), 0).astype(F32) + 1.0
    for j in range(chunks):
        ids = ids_ref[j * rows : (j + 1) * rows, :]
        used = jnp.max(jnp.where(ids >= 0.0, level, 0.0)).astype(jnp.int32)
        for i in range(rows):
            table[count + i] = j * rows + i
        count = count + used
    for i in range(BLOCK_ROWS):
        table[count + i] = chunks * rows
    table[table.shape[0] - 1] = lax.div(count + (BLOCK_ROWS - 1), BLOCK_ROWS)


def listed_rows(table, first, count):
    return [table[first + i] for i in range(count)]


def over_blocks(table, step):
    blocks = table[table.shape[0] - 1]
    done = jnp.int32(0)
    for size in TURNS:
        turns = lax.div(blocks - done, size)

        def turn(i, carry, done=done, size=size):
            step([done + i * size + u for u in range(size)])
            return carry

        lax.fori_loop(0, turns, turn, 0)
        done = done + turns * size


def stacked(field):
    high, low = split(field)
    top = jnp.concatenate([high, high], axis=1)
    bottom = jnp.concatenate([low, jnp.zeros_like(low)], axis=1)
    return jnp.concatenate([top, bottom], axis=0)


def forward_step(stack, phi, ids_row, row_iota, owned):
    both = jnp.dot(stack, phi, preferred_element_type=F32)
    value = both[:owned] + both[owned:]
    return jnp.sum(jnp.where(row_iota == ids_row, value, 0.0), axis=0, keepdims=True)


def store_rows(ref, rows, value):
    for i, r in enumerate(rows):
        ref[pl.ds(r, 1), :] = value[:, i * LANES : (i + 1) * LANES]


def basis_loop(table, ids_ref, time_ref, coef, phi_ref, value_ref):
    owned, terms = coef.shape
    half = terms // 2
    value_ref[...] = jnp.zeros(value_ref.shape, F32)
    width = STEP_LANES
    stack = stacked(coef)
    row_iota = lax.broadcasted_iota(jnp.int32, (owned, width), 0).astype(F32)
    fine = (lax.broadcasted_iota(jnp.int32, (8, width), 0) + 1).astype(F32)
    coarse = (lax.broadcasted_iota(jnp.int32, (half // 8, width), 0) * 8).astype(F32)

    def step(block, u):
        rows = listed_rows(table, block * BLOCK_ROWS + u * STEP_ROWS, STEP_ROWS)
        times = rows_pair(time_ref, rows)
        cos_fine, sin_fine = cos_sin_pi(fine * times)
        cos_coarse, sin_coarse = cos_sin_pi(coarse * times)
        cos_parts, sin_parts = [], []
        for j in range(half // 8):
            cj = cos_coarse[j : j + 1]
            sj = sin_coarse[j : j + 1]
            cos_parts.append(cj * cos_fine - sj * sin_fine)
            sin_parts.append(sj * cos_fine + cj * sin_fine)
        high, low = split(jnp.concatenate(cos_parts + sin_parts, axis=0))
        phi = jnp.concatenate([high, low], axis=0)
        phi_ref[block, :, u * width : (u + 1) * width] = phi
        value = forward_step(stack, phi, rows_pair(ids_ref, rows), row_iota, owned)
        store_rows(value_ref, rows, value)

    def whole_block(block, carry):
        for u in range(UNROLL):
            step(block, u)
        return carry

    lax.fori_loop(0, table[table.shape[0] - 1], whole_block, 0)


class Role:
    def __init__(self, sign, send, meta, phi, table, z_ref, value_ref, sum_ref, listed=False):
        if not listed:
            rows = (meta.shape[0] - DUMMY_ROWS) // send.shape[0]
            used_rows(meta, send.shape[0], rows, table)
        self.sign = sign
        self.table = table
        self.ids = meta
        self.phi = phi
        self.z_ref = z_ref
        self.value_ref = value_ref
        self.sum_ref = sum_ref
        self.count = meta.shape[0] - DUMMY_ROWS

    def cross(self, mine, other):
        return mine - other if self.sign > 0 else other - mine

    def backward(self, z, owned):
        high = z.astype(BF16).astype(F32)
        self.z_ref[0, : self.count] = high
        self.z_ref[1, : self.count] = z - high
        self.z_ref[:, self.count :] = jnp.zeros((2, DUMMY_ROWS, LANES), F32)
        blocks, double, width = self.phi.shape
        row_iota = lax.broadcasted_iota(jnp.int32, (owned, width), 0).astype(F32)

        def gather(block):
            rows = listed_rows(self.table, block * BLOCK_ROWS, BLOCK_ROWS)
            hit = row_iota == rows_pair(self.ids, rows)
            parts = [
                jnp.where(hit, rows_pair(self.z_ref.at[k], rows), 0.0).astype(BF16)
                for k in range(2)
            ]
            return lax.dot_general(
                jnp.concatenate(parts, axis=0),
                self.phi[block],
                (((1,), (1,)), ((), ())),
                preferred_element_type=F32,
            )

        return self.gathered(gather)

    def gathered(self, gather):
        self.sum_ref[...] = jnp.zeros(self.sum_ref.shape, F32)

        def step(blocks):
            self.sum_ref[...] += sum(gather(block) for block in blocks)

        over_blocks(self.table, step)
        g = self.sum_ref[...]
        owned, terms = g.shape[0] // 2, g.shape[1] // 2
        return self.sign * (g[:owned, :terms] + (g[:owned, terms:] + g[owned:, :terms]))

    def forward(self, field):
        owned = field.shape[0]
        stack = stacked(field)
        row_iota = lax.broadcasted_iota(jnp.int32, (owned, STEP_LANES), 0).astype(F32)
        self.value_ref[...] = jnp.zeros(self.value_ref.shape, F32)

        def ahead(block):
            for u in range(UNROLL):
                rows = listed_rows(self.table, block * BLOCK_ROWS + u * STEP_ROWS, STEP_ROWS)
                phi = self.phi[block, :, u * STEP_LANES : (u + 1) * STEP_LANES]
                value = forward_step(stack, phi, rows_pair(self.ids, rows), row_iota, owned)
                store_rows(self.value_ref, rows, value)

        def step(blocks):
            for block in blocks:
                ahead(block)

        over_blocks(self.table, step)
        return self.value_ref[: self.count]

    def forward_image(self, field, other, weight):
        owned = field.shape[0]
        stack = stacked(field)
        blocks, double, width = self.phi.shape
        row_iota = lax.broadcasted_iota(jnp.int32, (owned, width), 0).astype(F32)
        fill_padded(self.z_ref.at[0], other)
        fill_padded(self.z_ref.at[1], weight)
        self.value_ref[...] = jnp.zeros(self.value_ref.shape, F32)

        def both(block):
            rows = listed_rows(self.table, block * BLOCK_ROWS, BLOCK_ROWS)
            phi = self.phi[block]
            hit = row_iota == rows_pair(self.ids, rows)
            values = []
            for u in range(UNROLL):
                part = slice(u * STEP_LANES, (u + 1) * STEP_LANES)
                product = jnp.dot(stack, phi[:, part], preferred_element_type=F32)
                value = product[:owned] + product[owned:]
                values.append(
                    jnp.sum(jnp.where(hit[:, part], value, 0.0), axis=0, keepdims=True)
                )
            value = jnp.concatenate(values, axis=1)
            store_rows(self.value_ref, rows, value)
            z = rows_pair(self.z_ref.at[1], rows) * self.cross(
                value, rows_pair(self.z_ref.at[0], rows)
            )
            high = z.astype(BF16).astype(F32)
            parts = [jnp.where(hit, x, 0.0).astype(BF16) for x in (high, z - high)]
            return lax.dot_general(
                jnp.concatenate(parts, axis=0),
                phi,
                (((1,), (1,)), ((), ())),
                preferred_element_type=F32,
            )

        image = self.gathered(both)
        return self.value_ref[: self.count], SCALE * (image + damping * field)

    def weigh(self, residual):
        live = self.ids[: self.count] >= 0.0
        misfit = jnp.where(live, residual, 0.0)
        weight = jnp.where(live, 1.0 / (1.0 + misfit * misfit / cauchy_square), 0.0)
        return weight, weight * misfit

    def gradient(self, z, state):
        return self.backward(z, state.shape[0]) - damping * state

    def image(self, z, before):
        return SCALE * (self.backward(z, before.shape[0]) + damping * before)


def write_chunks(send, first, values):
    chunks, rows = send.shape[0], send.shape[2]
    for j in range(chunks):
        send[j, first] = values[j * rows : (j + 1) * rows, :]


def fill_padded(ref, values):
    count = values.shape[0]
    ref[:count] = values
    ref[count:] = jnp.zeros((ref.shape[0] - count,) + values.shape[1:], F32)


def setup_asc_kernel(
    fold, rows, packed, coef, meta, phi, state, short, onward, times, table, value_ref
):
    state[...] = coef[...]
    chunks = packed.shape[0] * fold
    count = chunks * rows
    meta[:count] = flat_first(packed, 0, fold, rows)
    meta[count:] = jnp.full((DUMMY_ROWS, LANES), -1.0, F32)
    fill_padded(times, flat_first(packed, 1, fold, rows))
    used_rows(meta, chunks, rows, table)
    basis_loop(table, meta, times, coef[...], phi, value_ref)
    short[...] = flat_first(packed, 4, fold, rows) - value_ref[:count]
    for j in range(chunks):
        base = j % fold * FIELDS
        for f in range(2):
            start = (base + f + 2) * rows
            onward[j, f * rows : (f + 1) * rows] = packed[j // fold, start : start + rows]
        onward[j, 2 * rows : 3 * rows] = short[j * rows : (j + 1) * rows]
        onward[j, 3 * rows :] = packed[j // fold, fold * FIELDS * rows :]


def setup_desc_kernel(
    fold, rows, packed, meta, phi, state, residual, weights, basis_0, value_0, send,
    times, table, z_ref, value_ref, sum_ref,
):
    chunks = packed.shape[0]
    count = chunks * rows
    home = lax.rem(lax.axis_index("asc"), fold) * (chunks // fold) + lax.axis_index("desc")
    state[...] = packed[home, 3 * rows :]
    meta[:count] = flat_second(packed, 0, rows)
    meta[count:] = jnp.full((DUMMY_ROWS, LANES), -1.0, F32)
    fill_padded(times, flat_second(packed, 1, rows))
    used_rows(meta, chunks, rows, table)
    basis_loop(table, meta, times, state[...], phi, value_ref)
    role = Role(-1.0, send, meta, phi, table, z_ref, value_ref, sum_ref, listed=True)
    own = value_ref[:count]
    write_chunks(send, 0, own)
    left = flat_second(packed, 2, rows) + own
    residual[...] = left
    weights[...], z = role.weigh(left)
    basis_0[...] = role.gradient(z, state[...])
    own = role.forward(basis_0[...])
    value_0[...] = own
    write_chunks(send, 1, own)


def first_asc_kernel(
    chunks, got, short, meta, phi, state,
    residual, weights, crossed_0, basis_0, basis_1, value_1, send, table, z_ref, value_ref, sum_ref,
):
    role = Role(1.0, send, meta, phi, table, z_ref, value_ref, sum_ref)
    left = short[...] + flat(got, 0, chunks)
    residual[...] = left
    weights[...], z = role.weigh(left)
    basis_0[...] = role.gradient(z, state[...])
    other = flat(got, 1, chunks)
    own, basis_1[...] = role.forward_image(basis_0[...], other, weights[...])
    write_chunks(send, 0, own)
    crossed_0[...] = role.cross(own, other)
    own = role.forward(basis_1[...])
    value_1[...] = own
    write_chunks(send, 1, own)


def images_kernel(sign, chunks, keep, got, value_0, meta, phi, weights, basis_0, *rest):
    basis_1, basis_2, send, *kept = rest[:-4]
    role = Role(sign, send, meta, phi, *rest[-4:])
    first = role.cross(value_0[...], flat(got, 0, chunks))
    basis_1[...] = role.image(weights[...] * first, basis_0[...])
    other = flat(got, 1, chunks)
    own, basis_2[...] = role.forward_image(basis_1[...], other, weights[...])
    write_chunks(send, 0, own)
    second = role.cross(own, other)
    own = role.forward(basis_2[...])
    write_chunks(send, 1, own)
    if keep:
        crossed_0, crossed_1, value_2 = kept
        crossed_0[...] = first
        crossed_1[...] = second
        value_2[...] = own


def total(x):
    return jnp.sum(jnp.sum(x, axis=0, keepdims=True), axis=1, keepdims=True)


PAIRS = [(0, 0), (0, 1), (0, 2), (1, 1), (1, 2), (2, 2)]


def gram_kernel(
    sign, chunks, keep, got, value_1, meta, phi, weights, crossed_0, basis_0, basis_1,
    other_0, other_1, other_2, *rest,
):
    basis_2, scalars, *kept = rest[:-4]
    role = Role(sign, got, meta, phi, *rest[-4:])
    weight = weights[...]
    crossed = role.cross(value_1[...], flat(got, 0, chunks))
    basis_2[...] = role.image(weight * crossed, basis_1[...])
    own = role.forward(basis_2[...])
    last = role.cross(own, flat(got, 1, chunks))
    if keep:
        crossed_1, crossed_2, value_2 = kept
        crossed_1[...] = crossed
        crossed_2[...] = last
        value_2[...] = own
    values = [crossed_0[...], crossed, last]
    mine = [basis_0[...], basis_1[...], basis_2[...]]
    others = [other_0[...], other_1[...], other_2[...]]
    lane = lax.broadcasted_iota(jnp.int32, (1, LANES), 1)
    line = jnp.zeros((1, LANES), F32)
    for place_in_line, (i, j) in enumerate(PAIRS):
        dots = total(mine[i] * mine[j] + others[i] * others[j])
        curve = total(weight * values[i] * values[j]) + damping * dots
        line = jnp.where(lane == place_in_line, curve, line)
        if i == 0:
            line = jnp.where(lane == len(PAIRS) + j, dots, line)
    for d in range(scalars.shape[0]):
        scalars[d] = line


def solve(scalars):
    summed = scalars[0]
    for d in range(1, scalars.shape[0]):
        summed = summed + scalars[d]
    line = summed
    lane = lax.broadcasted_iota(jnp.int32, (1, LANES), 1)

    def pick(place):
        return jnp.sum(jnp.where(lane == place, line, 0.0), axis=1, keepdims=True)

    g = {pair: pick(place) for place, pair in enumerate(PAIRS)}
    right = [pick(len(PAIRS) + i) for i in range(3)]
    s = [
        jnp.where(g[i, i] > 0.0, lax.rsqrt(jnp.maximum(g[i, i], 1e-37)), 0.0) for i in range(3)
    ]
    l10 = g[0, 1] * s[0] * s[1]
    l20 = g[0, 2] * s[0] * s[2]
    g21 = g[1, 2] * s[1] * s[2]
    c = [right[i] * s[i] for i in range(3)]

    def inverse(pivot):
        good = pivot > PIVOT_FLOOR
        return jnp.where(good, 1.0 / jnp.where(good, pivot, 1.0), 0.0)

    inv1 = inverse(1.0 - l10 * l10)
    t21 = g21 - l20 * l10
    l21 = t21 * inv1
    inv2 = inverse(1.0 - l20 * l20 - l21 * t21)
    u1 = c[1] - l10 * c[0]
    u2 = c[2] - l20 * c[0] - l21 * u1
    x2 = u2 * inv2
    x1 = u1 * inv1 - l21 * x2
    x0 = c[0] - l10 * x1 - l20 * x2
    return [x0 * s[0], x1 * s[1], x2 * s[2]]


def combine(y, parts):
    return y[0] * parts[0] + (y[1] * parts[1] + y[2] * parts[2])


def next_asc_kernel(
    chunks, scalars, meta, phi, residual, crossed_0, crossed_1, crossed_2,
    basis_a0, basis_a1, basis_a2, basis_d0, basis_d1, basis_d2, state_a, state_d, value_2,
    new_a, new_d, shares, weights, basis_0, value_0, send, table, z_ref, value_ref, sum_ref,
):
    role = Role(1.0, send, meta, phi, table, z_ref, value_ref, sum_ref)
    write_chunks(send, 0, value_2[...])
    y = solve(scalars)
    for i in range(3):
        shares[i : i + 1] = jnp.broadcast_to(y[i], (1, LANES))
    left = residual[...] - combine(y, [crossed_0[...], crossed_1[...], crossed_2[...]])
    new_a[...] = state_a[...] + combine(y, [basis_a0[...], basis_a1[...], basis_a2[...]])
    new_d[...] = state_d[...] + combine(y, [basis_d0[...], basis_d1[...], basis_d2[...]])
    weights[...], z = role.weigh(left)
    basis_0[...] = role.gradient(z, new_a[...])
    own = role.forward(basis_0[...])
    value_0[...] = own
    write_chunks(send, 1, own)


def next_desc_kernel(
    chunks, got, shares, meta, phi, residual, crossed_0, crossed_1, value_2, state,
    weights, new_crossed_0, basis_0, basis_1, value_1, send, table, z_ref, value_ref, sum_ref,
):
    role = Role(-1.0, send, meta, phi, table, z_ref, value_ref, sum_ref)
    y = [shares[i : i + 1] for i in range(3)]
    crossed_2 = role.cross(value_2[...], flat(got, 0, chunks))
    left = residual[...] - combine(y, [crossed_0[...], crossed_1[...], crossed_2])
    weights[...], z = role.weigh(left)
    basis_0[...] = role.gradient(z, state[...])
    other = flat(got, 1, chunks)
    own, basis_1[...] = role.forward_image(basis_0[...], other, weights[...])
    write_chunks(send, 0, own)
    new_crossed_0[...] = role.cross(own, other)
    own = role.forward(basis_1[...])
    value_1[...] = own
    write_chunks(send, 1, own)


def final_kernel(scalars, state_a, basis_0, basis_1, basis_2, desc, out_a, out_d):
    y = solve(scalars)
    out_a[...] = state_a[...] + combine(y, [basis_0[...], basis_1[...], basis_2[...]])
    out_d[...] = desc[0] + combine(y, [desc[1], desc[2], desc[3]])


def body(coef_asc, coef_desc, cross_asc, cross_desc, time_asc, time_desc, height, block_fill):
    owned_asc, terms = coef_asc.shape
    owned_desc = coef_desc.shape[0]
    blocks, width = cross_asc.shape
    na = lax.axis_size("asc")
    nd = lax.axis_size("desc")
    fold = na // nd
    rows = blocks * width // na // LANES
    all_rows = na * rows
    all_blocks = -(-all_rows // BLOCK_ROWS)
    shape = jax.ShapeDtypeStruct

    def call(kernel, outs, scratch, *args, in_specs=None, mebibytes=16):
        return pl.pallas_call(
            kernel,
            out_shape=outs,
            in_specs=[place(x) for x in args] if in_specs is None else in_specs,
            out_specs=jax.tree.map(place, outs),
            scratch_shapes=scratch,
            compiler_params=params(mebibytes),
        )(*args)

    to_role = []
    for p in range(na):
        for q in range(nd):
            to_role.append((p * nd + q, (q * fold + p // nd) * nd + p % nd))
    to_native = [(b, a) for a, b in to_role]
    slots = (cross_asc, cross_desc, time_asc, time_desc, height)
    packed = call(
        functools.partial(pack_kernel, na, nd, owned_asc),
        shape((nd, fold * FIELDS * rows + owned_desc, LANES), F32),
        [pltpu.VMEM(coef_desc.shape, F32)]
        + [pltpu.VMEM((blocks, width), x.dtype) for x in slots]
        + [
            pltpu.VMEM((1, blocks), jnp.int32),
            pltpu.VMEM((FIELDS, blocks, width), F32),
            pltpu.SemaphoreType.DMA((len(slots) + 2,)),
        ],
        coef_desc, *slots, block_fill.reshape(1, blocks),
        in_specs=[pl.BlockSpec(memory_space=pltpu.HBM)] * (len(slots) + 2),
        mebibytes=60,
    )
    at_asc = lax.all_to_all(packed, "desc", split_axis=0, concat_axis=0, tiled=True)

    padded = all_rows + DUMMY_ROWS
    meta_shape = shape((padded, LANES), F32)
    phi_shape = shape((all_blocks, 2 * terms, BLOCK_ROWS * LANES), BF16)
    role_shapes = [meta_shape, phi_shape]
    table = pltpu.SMEM((all_rows + rows + BLOCK_ROWS + 1,), jnp.int32)
    slot_shape = shape((all_rows, LANES), F32)
    send_shape = shape((na, 2, rows, LANES), F32)
    field_a = shape(coef_asc.shape, F32)
    field_d = shape(coef_desc.shape, F32)
    line_shape = shape((na * nd, 1, LANES), F32)
    times_scratch = pltpu.VMEM((padded, LANES), F32)
    scratch = [
        table, pltpu.VMEM((2, padded, LANES), F32), pltpu.VMEM((padded, LANES), F32),
        pltpu.VMEM((2 * owned_asc, 2 * terms), F32),
    ]

    def exchange(x):
        return lax.all_to_all(x, "asc", split_axis=0, concat_axis=0, tiled=True)

    def share(x):
        return lax.all_to_all(x, ("asc", "desc"), split_axis=0, concat_axis=0, tiled=True)

    *asc, state_a, short, onward = call(
        functools.partial(setup_asc_kernel, fold, rows),
        role_shapes + [field_a, slot_shape, shape((na, 3 * rows + owned_desc, LANES), F32)],
        [times_scratch, table, scratch[2]],
        at_asc, coef_asc,
    )
    *desc, state_d, residual_d, weights_d, d0, own_d, send = call(
        functools.partial(setup_desc_kernel, fold, rows),
        role_shapes + [field_d, slot_shape, slot_shape, field_d, slot_shape, send_shape],
        [times_scratch] + scratch,
        exchange(onward),
    )
    residual_a, weights_a, crossed_a0, a0, a1, own_a, send = call(
        functools.partial(first_asc_kernel, na),
        [slot_shape, slot_shape, slot_shape, field_a, field_a, slot_shape, send_shape],
        scratch,
        exchange(send), short, *asc, state_a,
    )
    kept = [slot_shape] * 3
    d1, d2, send, crossed_d0, crossed_d1, own_d = call(
        functools.partial(images_kernel, -1.0, na, True),
        [field_d, field_d, send_shape] + kept,
        scratch,
        exchange(send), own_d, *desc, weights_d, d0,
    )
    a2, scalars, crossed_a1, crossed_a2, own_a = call(
        functools.partial(gram_kernel, 1.0, na, True),
        [field_a, line_shape] + kept,
        scratch,
        exchange(send), own_a, *asc, weights_a, crossed_a0, a0, a1, d0, d1, d2,
    )
    state_a, state_d, shares, weights_a, a0, own_a, send = call(
        functools.partial(next_asc_kernel, na),
        [
            field_a, field_d, shape((8, LANES), F32),
            slot_shape, field_a, slot_shape, send_shape,
        ],
        scratch,
        share(scalars), *asc, residual_a, crossed_a0, crossed_a1, crossed_a2,
        a0, a1, a2, d0, d1, d2, state_a, state_d, own_a,
    )
    weights_d, crossed_d0, d0, d1, own_d, send = call(
        functools.partial(next_desc_kernel, na),
        [slot_shape, slot_shape, field_d, field_d, slot_shape, send_shape],
        scratch,
        exchange(send), shares, *desc, residual_d, crossed_d0, crossed_d1, own_d, state_d,
    )
    a1, a2, send = call(
        functools.partial(images_kernel, 1.0, na, False),
        [field_a, field_a, send_shape],
        scratch,
        exchange(send), own_a, *asc, weights_a, a0,
    )
    d2, scalars = call(
        functools.partial(gram_kernel, -1.0, na, False),
        [field_d, line_shape],
        scratch,
        exchange(send), own_d, *desc, weights_d, crossed_d0, d0, d1, a0, a1, a2,
    )
    leaving = jnp.stack([state_d, d0, d1, d2])
    native = lax.ppermute(leaving, ("asc", "desc"), to_native)
    return tuple(
        call(
            final_kernel,
            [field_a, field_d],
            [],
            share(scalars), state_a, a0, a1, a2, native,
        )
    )


def solution(mesh):
    split_rows = P(("asc", "desc"), None)
    return jax.shard_map(
        body,
        mesh=mesh,
        in_specs=(split_rows,) * 7 + (P(("asc", "desc")),),
        out_specs=(split_rows, split_rows),
        check_vma=False,
    )
```

profile of v0, /device:TPU:0, one launch (start us, length us, event | category | flops | bytes accessed | tf_op | source)
XLA Modules:
  0.0 117.3 jit_solution(17195266374514228977)
XLA Ops:
  0.6 2.2 %shard_map.95 = f32[4,112,128]{2,1,0:T(8,128)} custom-call(f32[32,128]{1,0:T(8,128)} %coef_in.1, s32[64,128]{1,0:T(8,128)} %ca_in.1, s32[64,128]{1,0:T(8,128)} %cd_in.1, f32[64,128]{1,0:T(8,128)} %ta_in.1, f32[64,128]{1,0:T(8,128)} %td_in.1, f32[64,128]{1,0:T(8,128)} %height_in.1, s32[1,64]{1,0:T(1,128)} %bitcast.9), custom_call_target="tpu_custom_call" | custom-call | tf_op jit(solution)/shard_map/pallas_call | solution.py:592
  2.8 14.5 %all_to_all.50.packed = f32[4,112,128]{2,1,0:T(8,128)S(1)} all-to-all(f32[4,112,128]{2,1,0:T(8,128)} %shard_map.95), channel_id=1, replica_groups=mesh['asc'=8,'desc'=4] {'desc'}, dimensions={0} | all-to-all | bytes 458752 | tf_op jit(solution)/shard_map/all_to_all | solution.py:621
  17.3 0.0 copy-start
  17.3 0.7 copy-done
  18.1 1.9 %shard_map.96 = (f32[72,128]{1,0:T(8,128)S(1)}, bf16[11,256,768]{2,1,0:T(8,128)(2,1)S(1)}, f32[32,128]{1,0:T(8,128)S(1)}, f32[64,128]{1,0:T(8,128)S(1)}, f32[8,56,128]{2,1,0:T(8,128)S(1)}) custom-call(f32[4,112,128]{2,1,0:T(8,128)S(1)} %all_to_all.50.packed, f32[32,128]{1,0:T(8,128)S(1)} %copy-done), custom_call_target="tpu_custom_call" | custom-call | tf_op jit(solution)/shard_map/pallas_call | solution.py:592
  19.9 10.1 %all_to_all.51.packed = f32[8,56,128]{2,1,0:T(8,128)S(1)} all-to-all(f32[8,56,128]{2,1,0:T(8,128)S(1)} %get-tuple-element.51), channel_id=1, replica_groups=mesh['asc'=8,'desc'=4] {'asc'}, dimensions={0} | all-to-all | bytes 458752 | tf_op jit(solution)/shard_map/all_to_all | solution.py:640
  30.0 3.1 %shard_map.97 = (f32[72,128]{1,0:T(8,128)S(1)}, bf16[11,256,768]{2,1,0:T(8,128)(2,1)S(1)}, f32[32,128]{1,0:T(8,128)S(1)}, f32[64,128]{1,0:T(8,128)S(1)}, f32[64,...) custom-call(f32[8,56,128]{2,1,0:T(8,128)S(1)} %all_to_all.51.packed), custom_call_target="tpu_custom_call" | custom-call | tf_op jit(solution)/shard_map/pallas_call | solution.py:592
  33.2 7.5 %all_to_all.52.got = f32[8,2,8,128]{3,2,1,0:T(8,128)S(1)} all-to-all(f32[8,2,8,128]{3,2,1,0:T(8,128)S(1)} %get-tuple-element.52), channel_id=1, replica_groups=mesh['asc'=8,'desc'=4] {'asc'}, dimensions={0} | all-to-all | bytes 131072 | tf_op jit(solution)/shard_map/all_to_all | solution.py:640
  40.6 2.9 %shard_map.98 = (f32[64,128]{1,0:T(8,128)S(1)}, f32[64,128]{1,0:T(8,128)S(1)}, f32[64,128]{1,0:T(8,128)S(1)}, f32[32,128]{1,0:T(8,128)S(1)}, f32[32,128]{1,0:T(8...) custom-call(f32[8,2,8,128]{3,2,1,0:T(8,128)S(1)} %all_to_all.52.got, ...), custom_call_target="tpu_custom_call" | custom-call | tf_op jit(solution)/shard_map/pallas_call | solution.py:592
  43.5 7.5 %all_to_all.53.got = f32[8,2,8,128]{3,2,1,0:T(8,128)S(1)} all-to-all(f32[8,2,8,128]{3,2,1,0:T(8,128)S(1)} %get-tuple-element.57), channel_id=1, replica_groups=mesh['asc'=8,'desc'=4] {'asc'}, dimensions={0} | all-to-all | bytes 131072 | tf_op jit(solution)/shard_map/all_to_all | solution.py:640
  51.0 2.9 %shard_map.99 = (f32[32,128]{1,0:T(8,128)S(1)}, f32[32,128]{1,0:T(8,128)S(1)}, f32[8,2,8,128]{3,2,1,0:T(8,128)S(1)}, f32[64,128]{1,0:T(8,128)S(1)}, f32[64,128]{1,0:T(8,128)S(1)}, /*index=5*/f32[64,128]{1,0:T(8,128)S(1)}) custom-call(f32[8,2,8,128]{3,2,1,0:T(8,128)S(1)} %all_to_all.53.got, f32[64,128]{1,0:T(8,128)S(1)} %get-tuple-element.58.value_0, ...), custom_call_target="tpu_custom_call" | custom-call | tf_op jit(solution)/shard_map/pallas_call | solution.py:592
  53.9 7.5 %all_to_all.54.got = f32[8,2,8,128]{3,2,1,0:T(8,128)S(1)} all-to-all(f32[8,2,8,128]{3,2,1,0:T(8,128)S(1)} %get-tuple-element.63), channel_id=1, replica_groups=mesh['asc'=8,'desc'=4] {'asc'}, dimensions={0} | all-to-all | bytes 131072 | tf_op jit(solution)/shard_map/all_to_all | solution.py:640
  61.4 1.6 %shard_map.100 = (f32[32,128]{1,0:T(8,128)S(1)}, f32[32,1,128]{2,1,0:T(1,128)S(1)}, f32[64,128]{1,0:T(8,128)S(1)}, f32[64,128]{1,0:T(8,128)S(1)}, f32[64,128]{1,0:T(8,128)S(1)}) custom-call(f32[8,2,8,128]{3,2,1,0:T(8,128)S(1)} %all_to_all.54.got, f32[64,128]{1,0:T(8,128)S(1)} %get-tuple-element.64.value_1, f32[72,128]{1,0:T(8,128)S(1)} %get-tuple-element.54.meta, ...), custom_call_target="tpu_custom_call" | custom-call | tf_op jit(solution)/shard_map/pallas_call | solution.py:592
  63.0 9.3 %all_to_all.55.scalars = f32[32,1,128]{2,1,0:T(1,128)S(1)} all-to-all(f32[32,1,128]{2,1,0:T(1,128)S(1)} %get-tuple-element.71), channel_id=1, replica_groups=mesh['asc'=8,'desc'=4] {'asc','desc'}, dimensions={0} | all-to-all | bytes 32768 | tf_op jit(solution)/shard_map/all_to_all | solution.py:643
  72.3 1.5 %shard_map.101 = (f32[32,128]{1,0:T(8,128)S(1)}, f32[32,128]{1,0:T(8,128)S(1)}, f32[8,128]{1,0:T(8,128)S(1)}, f32[64,128]{1,0:T(8,128)S(1)}, f32[32,128]{1,0:T(8...) custom-call(f32[32,1,128]{2,1,0:T(1,128)S(1)} %all_to_all.55.scalars, ...), custom_call_target="tpu_custom_call" | custom-call | tf_op jit(solution)/shard_map/pallas_call | solution.py:592
  73.8 7.4 %all_to_all.56.got = f32[8,2,8,128]{3,2,1,0:T(8,128)S(1)} all-to-all(f32[8,2,8,128]{3,2,1,0:T(8,128)S(1)} %get-tuple-element.78), channel_id=1, replica_groups=mesh['asc'=8,'desc'=4] {'asc'}, dimensions={0} | all-to-all | bytes 131072 | tf_op jit(solution)/shard_map/all_to_all | solution.py:640
  81.2 3.0 %shard_map.102 = (f32[64,128]{1,0:T(8,128)S(1)}, f32[64,128]{1,0:T(8,128)S(1)}, f32[32,128]{1,0:T(8,128)S(1)}, f32[32,128]{1,0:T(8,128)S(1)}, f32[64,128]{1,0:T(8,128)S(1)}, /*index=5*/f32[8,2,8,128]{3,2,1,0:T(8,128)S(1)}) custom-call(f32[8,2,8,128]{3,2,1,0:T(8,128)S(1)} %all_to_all.56.got, f32[8,128]{1,0:T(8,128)S(1)} %get-tuple-element.79.shares, ...), custom_call_target="tpu_custom_call" | custom-call | tf_op jit(solution)/shard_map/pallas_call | solution.py:592
  84.2 7.5 %all_to_all.57.got = f32[8,2,8,128]{3,2,1,0:T(8,128)S(1)} all-to-all(f32[8,2,8,128]{3,2,1,0:T(8,128)S(1)} %get-tuple-element.85), channel_id=1, replica_groups=mesh['asc'=8,'desc'=4] {'asc'}, dimensions={0} | all-to-all | bytes 131072 | tf_op jit(solution)/shard_map/all_to_all | solution.py:640
  91.7 2.9 %shard_map.103 = (f32[32,128]{1,0:T(8,128)S(1)}, f32[32,128]{1,0:T(8,128)S(1)}, f32[8,2,8,128]{3,2,1,0:T(8,128)S(1)}) custom-call(f32[8,2,8,128]{3,2,1,0:T(8,128)S(1)} %all_to_all.57.got, f32[64,128]{1,0:T(8,128)S(1)} %get-tuple-element.86.value_0, f32[72,128]{1,0:T(8,128)S(1)} %get-tuple-element.54.meta, bf16[11,256,768]{2,1,0:T(8,128)(2,1)S(1)} %get-tuple-element.55.phi, ...), custom_call_target="tpu_custom_call" | custom-call | tf_op jit(solution)/shard_map/pallas_call | solution.py:592
  94.6 7.5 %all_to_all.58.got = f32[8,2,8,128]{3,2,1,0:T(8,128)S(1)} all-to-all(f32[8,2,8,128]{3,2,1,0:T(8,128)S(1)} %get-tuple-element.89), channel_id=1, replica_groups=mesh['asc'=8,'desc'=4] {'asc'}, dimensions={0} | all-to-all | bytes 131072 | tf_op jit(solution)/shard_map/all_to_all | solution.py:640
  102.1 1.6 %shard_map.104 = (f32[32,128]{1,0:T(8,128)S(1)}, f32[32,1,128]{2,1,0:T(1,128)S(1)}) custom-call(f32[8,2,8,128]{3,2,1,0:T(8,128)S(1)} %all_to_all.58.got, f32[64,128]{1,0:T(8,128)S(1)} %get-tuple-element.90.value_1, f32[72,128]{1,0:T(8,128)S(1)} %get-tuple-element.59.meta, bf16[11,256,768]{2,1,0:T(8,128)(2,1)S(1)} %get-tuple-element.60.phi, ...), custom_call_target="tpu_custom_call" | custom-call | tf_op jit(solution)/shard_map/pallas_call | solution.py:592
  103.7 0.7 collective-permute-start
  104.4 12.2 %all_to_all.59.scalars = f32[32,1,128]{2,1,0:T(1,128)S(1)} all-to-all(f32[32,1,128]{2,1,0:T(1,128)S(1)} %get-tuple-element.97), channel_id=1, replica_groups=mesh['asc'=8,'desc'=4] {'asc','desc'}, dimensions={0} | all-to-all | bytes 32768 | tf_op jit(solution)/shard_map/all_to_all | solution.py:643
  116.5 0.0 collective-permute-done.desc
  116.6 0.8 shard_map.105
  (1 shorter events, 0.0 us)
Async XLA Ops:
  17.3 0.7 copy-start
  103.7 12.8 %collective-permute-start = (f32[4,32,128]{2,1,0:T(8,128)S(1)}, f32[4,32,128]{2,1,0:T(8,128)S(1)}, u32[]{:S(2)}, u32[]{:S(2)}) collective-permute-start(f32[4,32,128]{2,1,0:T(8,128)S(1)} %pad_maximum_fusion), channel_id=1, source_target_pairs={{0,0},{8,1},{16,2},{24,3},{1,4},{9,5},{17,6},{25,7},{2,8},{10,9},{... | collective-permute-start | bytes 196616 | tf_op jit(solution)/shard_map/ppermute | solution.py:705
where the time goes:
time: 118 us; the launch traced here: 117 us
  blocking collectives  91 us (77%)
  Pallas kernels  24.2 us (21%)
    all_to_all x7, blocking collectives, exchange(): return lax.all_to_all(x, 'asc', split_axis=0, concat_axis=0, tiled=True)  55.1 us
    pallas_call x11, Pallas kernels, call(): pl.pallas_call(kernel, out_shape=outs, in_specs=[place(x) for x in args]...  24.2 us
    all_to_all x2, blocking collectives, share(): lax.all_to_all(x, ('asc', 'desc'), split_axis=0, concat_axis=0, tiled=True)  21.4 us
    all_to_all x1, blocking collectives, body(): lax.all_to_all(packed, 'desc', split_axis=0, concat_axis=0, tiled=True)  14.5 us
  transfers between devices with their start and end apart: 1, of which 0 were waited for; matrix products, arithmetic and copies ran while one was open for 0% of the time, Pallas kernels for 0%

commit v1 on v0

--- a/solution.py
+++ b/solution.py
@@ -344,7 +344,7 @@
             )
 
         image = self.gathered(both)
-        return self.value_ref[: self.count], SCALE * (image + damping * field)
+        return self.value_ref[: self.count], SCALE * image
 
     def weigh(self, residual):
         live = self.ids[: self.count] >= 0.0
@@ -356,7 +356,7 @@
         return self.backward(z, state.shape[0]) - damping * state
 
     def image(self, z, before):
-        return SCALE * (self.backward(z, before.shape[0]) + damping * before)
+        return SCALE * self.backward(z, before.shape[0])
 
 
 def write_chunks(send, first, values):

time: 118 us -> 118 us (level)
  no operation moved by 1% of the time
where the time goes in v1:
time: 118 us; the launch traced here: 117 us
  blocking collectives  90.8 us (77%)
  Pallas kernels  24.2 us (21%)
    all_to_all x7, blocking collectives, exchange(): return lax.all_to_all(x, 'asc', split_axis=0, concat_axis=0, tiled=True)  55 us
    pallas_call x11, Pallas kernels, call(): pl.pallas_call(kernel, out_shape=outs, in_specs=[place(x) for x in args]...  24.2 us
    all_to_all x2, blocking collectives, share(): lax.all_to_all(x, ('asc', 'desc'), split_axis=0, concat_axis=0, tiled=True)  21.2 us
    all_to_all x1, blocking collectives, body(): lax.all_to_all(packed, 'desc', split_axis=0, concat_axis=0, tiled=True)  14.5 us
  transfers between devices with their start and end apart: 1, of which 0 were waited for; matrix products, arithmetic and copies ran while one was open for 0% of the time, Pallas kernels for 0%

profile of v1, /device:TPU:0, one launch (start us, length us, event | category | flops | bytes accessed | tf_op | source)
XLA Modules:
  0.0 117.1 jit_solution(10956982699801483627)
XLA Ops:
  0.6 2.2 %shard_map.95 = f32[4,112,128]{2,1,0:T(8,128)} custom-call(f32[32,128]{1,0:T(8,128)} %coef_in.1, s32[64,128]{1,0:T(8,128)} %ca_in.1, s32[64,128]{1,0:T(8,128)} %cd_in.1, f32[64,128]{1,0:T(8,128)} %ta_in.1, f32[64,128]{1,0:T(8,128)} %td_in.1, f32[64,128]{1,0:T(8,128)} %height_in.1, s32[1,64]{1,0:T(1,128)} %bitcast.9), custom_call_target="tpu_custom_call" | custom-call | tf_op jit(solution)/shard_map/pallas_call | solution.py:592
  2.8 14.5 %all_to_all.50.packed = f32[4,112,128]{2,1,0:T(8,128)S(1)} all-to-all(f32[4,112,128]{2,1,0:T(8,128)} %shard_map.95), channel_id=1, replica_groups=mesh['asc'=8,'desc'=4] {'desc'}, dimensions={0} | all-to-all | bytes 458752 | tf_op jit(solution)/shard_map/all_to_all | solution.py:621
  17.3 0.0 copy-start
  17.3 0.7 copy-done
  18.1 1.9 %shard_map.96 = (f32[72,128]{1,0:T(8,128)S(1)}, bf16[11,256,768]{2,1,0:T(8,128)(2,1)S(1)}, f32[32,128]{1,0:T(8,128)S(1)}, f32[64,128]{1,0:T(8,128)S(1)}, f32[8,56,128]{2,1,0:T(8,128)S(1)}) custom-call(f32[4,112,128]{2,1,0:T(8,128)S(1)} %all_to_all.50.packed, f32[32,128]{1,0:T(8,128)S(1)} %copy-done), custom_call_target="tpu_custom_call" | custom-call | tf_op jit(solution)/shard_map/pallas_call | solution.py:592
  19.9 10.1 %all_to_all.51.packed = f32[8,56,128]{2,1,0:T(8,128)S(1)} all-to-all(f32[8,56,128]{2,1,0:T(8,128)S(1)} %get-tuple-element.51), channel_id=1, replica_groups=mesh['asc'=8,'desc'=4] {'asc'}, dimensions={0} | all-to-all | bytes 458752 | tf_op jit(solution)/shard_map/all_to_all | solution.py:640
  30.0 3.1 %shard_map.97 = (f32[72,128]{1,0:T(8,128)S(1)}, bf16[11,256,768]{2,1,0:T(8,128)(2,1)S(1)}, f32[32,128]{1,0:T(8,128)S(1)}, f32[64,128]{1,0:T(8,128)S(1)}, f32[64,...) custom-call(f32[8,56,128]{2,1,0:T(8,128)S(1)} %all_to_all.51.packed), custom_call_target="tpu_custom_call" | custom-call | tf_op jit(solution)/shard_map/pallas_call | solution.py:592
  33.2 7.5 %all_to_all.52.got = f32[8,2,8,128]{3,2,1,0:T(8,128)S(1)} all-to-all(f32[8,2,8,128]{3,2,1,0:T(8,128)S(1)} %get-tuple-element.52), channel_id=1, replica_groups=mesh['asc'=8,'desc'=4] {'asc'}, dimensions={0} | all-to-all | bytes 131072 | tf_op jit(solution)/shard_map/all_to_all | solution.py:640
  40.6 2.9 %shard_map.98 = (f32[64,128]{1,0:T(8,128)S(1)}, f32[64,128]{1,0:T(8,128)S(1)}, f32[64,128]{1,0:T(8,128)S(1)}, f32[32,128]{1,0:T(8,128)S(1)}, f32[32,128]{1,0:T(8...) custom-call(f32[8,2,8,128]{3,2,1,0:T(8,128)S(1)} %all_to_all.52.got, ...), custom_call_target="tpu_custom_call" | custom-call | tf_op jit(solution)/shard_map/pallas_call | solution.py:592
  43.5 7.5 %all_to_all.53.got = f32[8,2,8,128]{3,2,1,0:T(8,128)S(1)} all-to-all(f32[8,2,8,128]{3,2,1,0:T(8,128)S(1)} %get-tuple-element.57), channel_id=1, replica_groups=mesh['asc'=8,'desc'=4] {'asc'}, dimensions={0} | all-to-all | bytes 131072 | tf_op jit(solution)/shard_map/all_to_all | solution.py:640
  51.0 2.9 %shard_map.99 = (f32[32,128]{1,0:T(8,128)S(1)}, f32[32,128]{1,0:T(8,128)S(1)}, f32[8,2,8,128]{3,2,1,0:T(8,128)S(1)}, f32[64,128]{1,0:T(8,128)S(1)}, f32[64,128]{1,0:T(8,128)S(1)}, /*index=5*/f32[64,128]{1,0:T(8,128)S(1)}) custom-call(f32[8,2,8,128]{3,2,1,0:T(8,128)S(1)} %all_to_all.53.got, f32[64,128]{1,0:T(8,128)S(1)} %get-tuple-element.58.value_0, ...), custom_call_target="tpu_custom_call" | custom-call | tf_op jit(solution)/shard_map/pallas_call | solution.py:592
  53.9 7.5 %all_to_all.54.got = f32[8,2,8,128]{3,2,1,0:T(8,128)S(1)} all-to-all(f32[8,2,8,128]{3,2,1,0:T(8,128)S(1)} %get-tuple-element.63), channel_id=1, replica_groups=mesh['asc'=8,'desc'=4] {'asc'}, dimensions={0} | all-to-all | bytes 131072 | tf_op jit(solution)/shard_map/all_to_all | solution.py:640
  61.4 1.6 %shard_map.100 = (f32[32,128]{1,0:T(8,128)S(1)}, f32[32,1,128]{2,1,0:T(1,128)S(1)}, f32[64,128]{1,0:T(8,128)S(1)}, f32[64,128]{1,0:T(8,128)S(1)}, f32[64,128]{1,0:T(8,128)S(1)}) custom-call(f32[8,2,8,128]{3,2,1,0:T(8,128)S(1)} %all_to_all.54.got, f32[64,128]{1,0:T(8,128)S(1)} %get-tuple-element.64.value_1, f32[72,128]{1,0:T(8,128)S(1)} %get-tuple-element.54.meta, ...), custom_call_target="tpu_custom_call" | custom-call | tf_op jit(solution)/shard_map/pallas_call | solution.py:592
  63.0 9.3 %all_to_all.55.scalars = f32[32,1,128]{2,1,0:T(1,128)S(1)} all-to-all(f32[32,1,128]{2,1,0:T(1,128)S(1)} %get-tuple-element.71), channel_id=1, replica_groups=mesh['asc'=8,'desc'=4] {'asc','desc'}, dimensions={0} | all-to-all | bytes 32768 | tf_op jit(solution)/shard_map/all_to_all | solution.py:643
  72.3 1.5 %shard_map.101 = (f32[32,128]{1,0:T(8,128)S(1)}, f32[32,128]{1,0:T(8,128)S(1)}, f32[8,128]{1,0:T(8,128)S(1)}, f32[64,128]{1,0:T(8,128)S(1)}, f32[32,128]{1,0:T(8...) custom-call(f32[32,1,128]{2,1,0:T(1,128)S(1)} %all_to_all.55.scalars, ...), custom_call_target="tpu_custom_call" | custom-call | tf_op jit(solution)/shard_map/pallas_call | solution.py:592
  73.7 7.4 %all_to_all.56.got = f32[8,2,8,128]{3,2,1,0:T(8,128)S(1)} all-to-all(f32[8,2,8,128]{3,2,1,0:T(8,128)S(1)} %get-tuple-element.78), channel_id=1, replica_groups=mesh['asc'=8,'desc'=4] {'asc'}, dimensions={0} | all-to-all | bytes 131072 | tf_op jit(solution)/shard_map/all_to_all | solution.py:640
  81.1 3.0 %shard_map.102 = (f32[64,128]{1,0:T(8,128)S(1)}, f32[64,128]{1,0:T(8,128)S(1)}, f32[32,128]{1,0:T(8,128)S(1)}, f32[32,128]{1,0:T(8,128)S(1)}, f32[64,128]{1,0:T(8,128)S(1)}, /*index=5*/f32[8,2,8,128]{3,2,1,0:T(8,128)S(1)}) custom-call(f32[8,2,8,128]{3,2,1,0:T(8,128)S(1)} %all_to_all.56.got, f32[8,128]{1,0:T(8,128)S(1)} %get-tuple-element.79.shares, ...), custom_call_target="tpu_custom_call" | custom-call | tf_op jit(solution)/shard_map/pallas_call | solution.py:592
  84.2 7.5 %all_to_all.57.got = f32[8,2,8,128]{3,2,1,0:T(8,128)S(1)} all-to-all(f32[8,2,8,128]{3,2,1,0:T(8,128)S(1)} %get-tuple-element.85), channel_id=1, replica_groups=mesh['asc'=8,'desc'=4] {'asc'}, dimensions={0} | all-to-all | bytes 131072 | tf_op jit(solution)/shard_map/all_to_all | solution.py:640
  91.7 2.9 %shard_map.103 = (f32[32,128]{1,0:T(8,128)S(1)}, f32[32,128]{1,0:T(8,128)S(1)}, f32[8,2,8,128]{3,2,1,0:T(8,128)S(1)}) custom-call(f32[8,2,8,128]{3,2,1,0:T(8,128)S(1)} %all_to_all.57.got, f32[64,128]{1,0:T(8,128)S(1)} %get-tuple-element.86.value_0, f32[72,128]{1,0:T(8,128)S(1)} %get-tuple-element.54.meta, bf16[11,256,768]{2,1,0:T(8,128)(2,1)S(1)} %get-tuple-element.55.phi, ...), custom_call_target="tpu_custom_call" | custom-call | tf_op jit(solution)/shard_map/pallas_call | solution.py:592
  94.6 7.5 %all_to_all.58.got = f32[8,2,8,128]{3,2,1,0:T(8,128)S(1)} all-to-all(f32[8,2,8,128]{3,2,1,0:T(8,128)S(1)} %get-tuple-element.89), channel_id=1, replica_groups=mesh['asc'=8,'desc'=4] {'asc'}, dimensions={0} | all-to-all | bytes 131072 | tf_op jit(solution)/shard_map/all_to_all | solution.py:640
  102.1 1.6 %shard_map.104 = (f32[32,128]{1,0:T(8,128)S(1)}, f32[32,1,128]{2,1,0:T(1,128)S(1)}) custom-call(f32[8,2,8,128]{3,2,1,0:T(8,128)S(1)} %all_to_all.58.got, f32[64,128]{1,0:T(8,128)S(1)} %get-tuple-element.90.value_1, f32[72,128]{1,0:T(8,128)S(1)} %get-tuple-element.59.meta, bf16[11,256,768]{2,1,0:T(8,128)(2,1)S(1)} %get-tuple-element.60.phi, ...), custom_call_target="tpu_custom_call" | custom-call | tf_op jit(solution)/shard_map/pallas_call | solution.py:592
  103.7 0.7 collective-permute-start
  104.4 12.0 %all_to_all.59.scalars = f32[32,1,128]{2,1,0:T(1,128)S(1)} all-to-all(f32[32,1,128]{2,1,0:T(1,128)S(1)} %get-tuple-element.97), channel_id=1, replica_groups=mesh['asc'=8,'desc'=4] {'asc','desc'}, dimensions={0} | all-to-all | bytes 32768 | tf_op jit(solution)/shard_map/all_to_all | solution.py:643
  116.3 0.0 collective-permute-done.desc
  116.3 0.8 shard_map.105
  (1 shorter events, 0.0 us)
Async XLA Ops:
  17.3 0.7 copy-start
  103.7 12.6 %collective-permute-start = (f32[4,32,128]{2,1,0:T(8,128)S(1)}, f32[4,32,128]{2,1,0:T(8,128)S(1)}, u32[]{:S(2)}, u32[]{:S(2)}) collective-permute-start(f32[4,32,128]{2,1,0:T(8,128)S(1)} %pad_maximum_fusion), channel_id=1, source_target_pairs={{0,0},{8,1},{16,2},{24,3},{1,4},{9,5},{17,6},{25,7},{2,8},{10,9},{... | collective-permute-start | bytes 196616 | tf_op jit(solution)/shard_map/ppermute | solution.py:705

commit v2 on v1

--- a/solution.py
+++ b/solution.py
@@ -107,16 +107,19 @@
     owner = target // group
     place = target - owner * group
     order = (source == place * na + owner).astype(F32).astype(BF16)
-    for f, field in enumerate(fields):
+    pieces = []
+    for field in fields:
         x = field()
         high = x.astype(BF16)
         rest = x - high.astype(F32)
         middle = rest.astype(BF16)
-        low = (rest - middle.astype(F32)).astype(BF16)
-        turned[f] = (
-            jnp.dot(high, order, preferred_element_type=F32)
-            + jnp.dot(middle, order, preferred_element_type=F32)
-        ) + jnp.dot(low, order, preferred_element_type=F32)
+        pieces += [high, middle, (rest - middle.astype(F32)).astype(BF16)]
+    product = jnp.dot(jnp.concatenate(pieces, axis=0), order, preferred_element_type=F32)
+    for f in range(FIELDS):
+        high, middle, low = [
+            product[(3 * f + k) * blocks : (3 * f + k + 1) * blocks] for k in range(3)
+        ]
+        turned[f] = (high + middle) + low
     lane_group = lax.broadcasted_iota(jnp.int32, (rows, width), 1) // group
     for f in range(FIELDS):
         parts = [None] * na

time: 118 us -> 119 us (level); the launches traced: 117 us -> 117 us
  no operation moved by 1% of the time
where the time goes in v2:
time: 119 us; the launch traced here: 117 us
  blocking collectives  90.3 us (76%)
  Pallas kernels  24.2 us (20%)
    all_to_all x7, blocking collectives, exchange(): return lax.all_to_all(x, 'asc', split_axis=0, concat_axis=0, tiled=True)  54.8 us
    pallas_call x11, Pallas kernels, call(): pl.pallas_call(kernel, out_shape=outs, in_specs=[place(x) for x in args]...  24.2 us
    all_to_all x2, blocking collectives, share(): lax.all_to_all(x, ('asc', 'desc'), split_axis=0, concat_axis=0, tiled=True)  21 us
    all_to_all x1, blocking collectives, body(): lax.all_to_all(packed, 'desc', split_axis=0, concat_axis=0, tiled=True)  14.5 us
  transfers between devices with their start and end apart: 1, of which 0 were waited for; matrix products, arithmetic and copies ran while one was open for 0% of the time, Pallas kernels for 0%

profile of v2, /device:TPU:0, one launch (start us, length us, event | category | flops | bytes accessed | tf_op | source)
XLA Modules:
  0.0 116.6 jit_solution(10112917180714520456)
XLA Ops:
  0.6 2.2 %shard_map.95 = f32[4,112,128]{2,1,0:T(8,128)} custom-call(f32[32,128]{1,0:T(8,128)} %coef_in.1, s32[64,128]{1,0:T(8,128)} %ca_in.1, s32[64,128]{1,0:T(8,128)} %cd_in.1, f32[64,128]{1,0:T(8,128)} %ta_in.1, f32[64,128]{1,0:T(8,128)} %td_in.1, f32[64,128]{1,0:T(8,128)} %height_in.1, s32[1,64]{1,0:T(1,128)} %bitcast.9), custom_call_target="tpu_custom_call" | custom-call | tf_op jit(solution)/shard_map/pallas_call | solution.py:595
  2.8 14.5 %all_to_all.50.packed = f32[4,112,128]{2,1,0:T(8,128)S(1)} all-to-all(f32[4,112,128]{2,1,0:T(8,128)} %shard_map.95), channel_id=1, replica_groups=mesh['asc'=8,'desc'=4] {'desc'}, dimensions={0} | all-to-all | bytes 458752 | tf_op jit(solution)/shard_map/all_to_all | solution.py:624
  17.3 0.0 copy-start
  17.3 0.7 copy-done
  18.1 1.9 %shard_map.96 = (f32[72,128]{1,0:T(8,128)S(1)}, bf16[11,256,768]{2,1,0:T(8,128)(2,1)S(1)}, f32[32,128]{1,0:T(8,128)S(1)}, f32[64,128]{1,0:T(8,128)S(1)}, f32[8,56,128]{2,1,0:T(8,128)S(1)}) custom-call(f32[4,112,128]{2,1,0:T(8,128)S(1)} %all_to_all.50.packed, f32[32,128]{1,0:T(8,128)S(1)} %copy-done), custom_call_target="tpu_custom_call" | custom-call | tf_op jit(solution)/shard_map/pallas_call | solution.py:595
  19.9 10.1 %all_to_all.51.packed = f32[8,56,128]{2,1,0:T(8,128)S(1)} all-to-all(f32[8,56,128]{2,1,0:T(8,128)S(1)} %get-tuple-element.51), channel_id=1, replica_groups=mesh['asc'=8,'desc'=4] {'asc'}, dimensions={0} | all-to-all | bytes 458752 | tf_op jit(solution)/shard_map/all_to_all | solution.py:643
  30.0 3.1 %shard_map.97 = (f32[72,128]{1,0:T(8,128)S(1)}, bf16[11,256,768]{2,1,0:T(8,128)(2,1)S(1)}, f32[32,128]{1,0:T(8,128)S(1)}, f32[64,128]{1,0:T(8,128)S(1)}, f32[64,...) custom-call(f32[8,56,128]{2,1,0:T(8,128)S(1)} %all_to_all.51.packed), custom_call_target="tpu_custom_call" | custom-call | tf_op jit(solution)/shard_map/pallas_call | solution.py:595
  33.2 7.5 %all_to_all.52.got = f32[8,2,8,128]{3,2,1,0:T(8,128)S(1)} all-to-all(f32[8,2,8,128]{3,2,1,0:T(8,128)S(1)} %get-tuple-element.52), channel_id=1, replica_groups=mesh['asc'=8,'desc'=4] {'asc'}, dimensions={0} | all-to-all | bytes 131072 | tf_op jit(solution)/shard_map/all_to_all | solution.py:643
  40.6 2.9 %shard_map.98 = (f32[64,128]{1,0:T(8,128)S(1)}, f32[64,128]{1,0:T(8,128)S(1)}, f32[64,128]{1,0:T(8,128)S(1)}, f32[32,128]{1,0:T(8,128)S(1)}, f32[32,128]{1,0:T(8...) custom-call(f32[8,2,8,128]{3,2,1,0:T(8,128)S(1)} %all_to_all.52.got, ...), custom_call_target="tpu_custom_call" | custom-call | tf_op jit(solution)/shard_map/pallas_call | solution.py:595
  43.5 7.4 %all_to_all.53.got = f32[8,2,8,128]{3,2,1,0:T(8,128)S(1)} all-to-all(f32[8,2,8,128]{3,2,1,0:T(8,128)S(1)} %get-tuple-element.57), channel_id=1, replica_groups=mesh['asc'=8,'desc'=4] {'asc'}, dimensions={0} | all-to-all | bytes 131072 | tf_op jit(solution)/shard_map/all_to_all | solution.py:643
  50.9 2.9 %shard_map.99 = (f32[32,128]{1,0:T(8,128)S(1)}, f32[32,128]{1,0:T(8,128)S(1)}, f32[8,2,8,128]{3,2,1,0:T(8,128)S(1)}, f32[64,128]{1,0:T(8,128)S(1)}, f32[64,128]{1,0:T(8,128)S(1)}, /*index=5*/f32[64,128]{1,0:T(8,128)S(1)}) custom-call(f32[8,2,8,128]{3,2,1,0:T(8,128)S(1)} %all_to_all.53.got, f32[64,128]{1,0:T(8,128)S(1)} %get-tuple-element.58.value_0, ...), custom_call_target="tpu_custom_call" | custom-call | tf_op jit(solution)/shard_map/pallas_call | solution.py:595
  53.8 7.5 %all_to_all.54.got = f32[8,2,8,128]{3,2,1,0:T(8,128)S(1)} all-to-all(f32[8,2,8,128]{3,2,1,0:T(8,128)S(1)} %get-tuple-element.63), channel_id=1, replica_groups=mesh['asc'=8,'desc'=4] {'asc'}, dimensions={0} | all-to-all | bytes 131072 | tf_op jit(solution)/shard_map/all_to_all | solution.py:643
  61.3 1.6 %shard_map.100 = (f32[32,128]{1,0:T(8,128)S(1)}, f32[32,1,128]{2,1,0:T(1,128)S(1)}, f32[64,128]{1,0:T(8,128)S(1)}, f32[64,128]{1,0:T(8,128)S(1)}, f32[64,128]{1,0:T(8,128)S(1)}) custom-call(f32[8,2,8,128]{3,2,1,0:T(8,128)S(1)} %all_to_all.54.got, f32[64,128]{1,0:T(8,128)S(1)} %get-tuple-element.64.value_1, f32[72,128]{1,0:T(8,128)S(1)} %get-tuple-element.54.meta, ...), custom_call_target="tpu_custom_call" | custom-call | tf_op jit(solution)/shard_map/pallas_call | solution.py:595
  62.9 8.9 %all_to_all.55.scalars = f32[32,1,128]{2,1,0:T(1,128)S(1)} all-to-all(f32[32,1,128]{2,1,0:T(1,128)S(1)} %get-tuple-element.71), channel_id=1, replica_groups=mesh['asc'=8,'desc'=4] {'asc','desc'}, dimensions={0} | all-to-all | bytes 32768 | tf_op jit(solution)/shard_map/all_to_all | solution.py:646
  71.7 1.5 %shard_map.101 = (f32[32,128]{1,0:T(8,128)S(1)}, f32[32,128]{1,0:T(8,128)S(1)}, f32[8,128]{1,0:T(8,128)S(1)}, f32[64,128]{1,0:T(8,128)S(1)}, f32[32,128]{1,0:T(8...) custom-call(f32[32,1,128]{2,1,0:T(1,128)S(1)} %all_to_all.55.scalars, ...), custom_call_target="tpu_custom_call" | custom-call | tf_op jit(solution)/shard_map/pallas_call | solution.py:595
  73.2 7.4 %all_to_all.56.got = f32[8,2,8,128]{3,2,1,0:T(8,128)S(1)} all-to-all(f32[8,2,8,128]{3,2,1,0:T(8,128)S(1)} %get-tuple-element.78), channel_id=1, replica_groups=mesh['asc'=8,'desc'=4] {'asc'}, dimensions={0} | all-to-all | bytes 131072 | tf_op jit(solution)/shard_map/all_to_all | solution.py:643
  80.6 3.1 %shard_map.102 = (f32[64,128]{1,0:T(8,128)S(1)}, f32[64,128]{1,0:T(8,128)S(1)}, f32[32,128]{1,0:T(8,128)S(1)}, f32[32,128]{1,0:T(8,128)S(1)}, f32[64,128]{1,0:T(8,128)S(1)}, /*index=5*/f32[8,2,8,128]{3,2,1,0:T(8,128)S(1)}) custom-call(f32[8,2,8,128]{3,2,1,0:T(8,128)S(1)} %all_to_all.56.got, f32[8,128]{1,0:T(8,128)S(1)} %get-tuple-element.79.shares, ...), custom_call_target="tpu_custom_call" | custom-call | tf_op jit(solution)/shard_map/pallas_call | solution.py:595
  83.7 7.5 %all_to_all.57.got = f32[8,2,8,128]{3,2,1,0:T(8,128)S(1)} all-to-all(f32[8,2,8,128]{3,2,1,0:T(8,128)S(1)} %get-tuple-element.85), channel_id=1, replica_groups=mesh['asc'=8,'desc'=4] {'asc'}, dimensions={0} | all-to-all | bytes 131072 | tf_op jit(solution)/shard_map/all_to_all | solution.py:643
  91.2 2.9 %shard_map.103 = (f32[32,128]{1,0:T(8,128)S(1)}, f32[32,128]{1,0:T(8,128)S(1)}, f32[8,2,8,128]{3,2,1,0:T(8,128)S(1)}) custom-call(f32[8,2,8,128]{3,2,1,0:T(8,128)S(1)} %all_to_all.57.got, f32[64,128]{1,0:T(8,128)S(1)} %get-tuple-element.86.value_0, f32[72,128]{1,0:T(8,128)S(1)} %get-tuple-element.54.meta, bf16[11,256,768]{2,1,0:T(8,128)(2,1)S(1)} %get-tuple-element.55.phi, ...), custom_call_target="tpu_custom_call" | custom-call | tf_op jit(solution)/shard_map/pallas_call | solution.py:595
  94.1 7.4 %all_to_all.58.got = f32[8,2,8,128]{3,2,1,0:T(8,128)S(1)} all-to-all(f32[8,2,8,128]{3,2,1,0:T(8,128)S(1)} %get-tuple-element.89), channel_id=1, replica_groups=mesh['asc'=8,'desc'=4] {'asc'}, dimensions={0} | all-to-all | bytes 131072 | tf_op jit(solution)/shard_map/all_to_all | solution.py:643
  101.5 1.6 %shard_map.104 = (f32[32,128]{1,0:T(8,128)S(1)}, f32[32,1,128]{2,1,0:T(1,128)S(1)}) custom-call(f32[8,2,8,128]{3,2,1,0:T(8,128)S(1)} %all_to_all.58.got, f32[64,128]{1,0:T(8,128)S(1)} %get-tuple-element.90.value_1, f32[72,128]{1,0:T(8,128)S(1)} %get-tuple-element.59.meta, bf16[11,256,768]{2,1,0:T(8,128)(2,1)S(1)} %get-tuple-element.60.phi, ...), custom_call_target="tpu_custom_call" | custom-call | tf_op jit(solution)/shard_map/pallas_call | solution.py:595
  103.1 0.7 collective-permute-start
  103.7 12.1 %all_to_all.59.scalars = f32[32,1,128]{2,1,0:T(1,128)S(1)} all-to-all(f32[32,1,128]{2,1,0:T(1,128)S(1)} %get-tuple-element.97), channel_id=1, replica_groups=mesh['asc'=8,'desc'=4] {'asc','desc'}, dimensions={0} | all-to-all | bytes 32768 | tf_op jit(solution)/shard_map/all_to_all | solution.py:646
  115.9 0.0 collective-permute-done.desc
  115.9 0.8 shard_map.105
  (1 shorter events, 0.0 us)
Async XLA Ops:
  17.3 0.7 copy-start
  103.1 12.8 %collective-permute-start = (f32[4,32,128]{2,1,0:T(8,128)S(1)}, f32[4,32,128]{2,1,0:T(8,128)S(1)}, u32[]{:S(2)}, u32[]{:S(2)}) collective-permute-start(f32[4,32,128]{2,1,0:T(8,128)S(1)} %pad_maximum_fusion), channel_id=1, source_target_pairs={{0,0},{8,1},{16,2},{24,3},{1,4},{9,5},{17,6},{25,7},{2,8},{10,9},{... | collective-permute-start | bytes 196616 | tf_op jit(solution)/shard_map/ppermute | solution.py:708
